TPU v7x, 32 devices: a whole 2x2x4 slice. The times are simulated.
32 devices in a mesh: groups: 2 (over y), blk: 8 (over z, x), dim: 2 (over core).
Axes of the slice: x: 2, y: 2, z: 4, core: 2. Of those that a mesh axis runs over, the one named last changes fastest.
Arguments:
- queries: bfloat16 [128, 8192], P('blk', 'dim'), may hold values from -6 to 6
- train_proj: bfloat16 [6144, 8192], P(('groups', 'blk'), 'dim'), parts along dimension 0, may hold values from -6 to 6
- basis: bfloat16 [64, 128, 128], P('dim'), may hold values from -0.5 to 0.5
- inv_eigen: float32 [64, 128], P('dim'), may hold values from 0.1 to 3
Outputs:
- scores: float32 [128, 6144], P(None, ('groups', 'blk', 'dim')), parts along dimension 1
There are 2 independent parts, one for each index of `groups`. A program takes and returns all parts, laid end to end along the dimension named above; an argument that names none is the same for every part. Nothing has to cross between parts.
All inputs are finite; a program needn't handle non-finite values.
Results may differ from a plain program's by a relative error of at most 0.0037.
Values may be sent and summed in bfloat16 or wider, within the bound.
A program may use at most 64 MiB of HBM per device.

v0:
```python
import jax
import jax.numpy as jnp
from jax import lax
from jax.sharding import PartitionSpec as P

PROJ = 8192


def precondition(queries, basis, inv_eigen):
    count = queries.shape[0]
    local_modules = basis.shape[0]
    width = basis.shape[1]
    blocks = queries.reshape(count, local_modules, width)
    rotated = (
        jnp.einsum("qmb,mbc->qmc", blocks, basis, preferred_element_type=jnp.float32)
        * inv_eigen[None, :, :]
    )
    rotated = rotated.astype(jnp.bfloat16)
    precond = jnp.einsum("qmc,mbc->qmb", rotated, basis, preferred_element_type=jnp.float32).astype(
        jnp.bfloat16
    )
    return precond.reshape(count, local_modules * width)


def shards(queries, train_proj, basis, inv_eigen):
    precond = precondition(queries, basis, inv_eigen)
    factor = 1.0 / jnp.sqrt(jnp.float32(PROJ))
    terms = lax.dot_general(
        lax.all_gather(precond, "blk", axis=0, tiled=True),
        train_proj,
        (((1,), (1,)), ((), ())),
        preferred_element_type=jnp.float32,
    )
    half = train_proj.shape[0] // lax.axis_size("dim")
    summed = lax.psum(terms, "dim")
    own = lax.dynamic_slice_in_dim(summed, lax.axis_index("dim") * half, half, 1)
    return own * factor


def solution(mesh):
    placed = (P("blk", "dim"), P(("groups", "blk"), "dim"), P("dim", None, None), P("dim", None))
    return jax.shard_map(
        shards,
        mesh=mesh,
        in_specs=placed,
        out_specs=P(None, ("groups", "blk", "dim")),
        check_vma=False,
    )
```

profile of v0, /device:TPU:0, one launch (start us, length us, event | category | flops | bytes accessed | tf_op | source)
XLA Modules:
  0.0 81.2 jit_solution(14227312706884130472)
XLA Ops:
  6.5 0.0 copy-start
  6.5 0.0 all-gather.2.cloned.1.call-start
  6.5 2.7 %fusion.1 = bf16[32,2,8,128]{3,2,1,0:T(8,128)(2,1)S(1)} fusion(bf16[32,128,128]{2,1,0:T(8,128)(2,1)} %param.6, f32[32,128]{1,0:T(8,128)} %param.7, bf16[16,4096]{1,0:T(8,128)(2,1)} %param.4), kind=kOutput, calls=%fused_computation.3 | convolution fusion | flops 33751040 | bytes 1327104 | tf_op jit(solution)/shard_map/qmc,mbc->qmb/dot_general | solution.py:19
  9.2 0.7 copy.15
  9.9 0.0 all-gather.2.cloned.1.call-update
  9.9 0.0 all-reduce.2.cloned.1.call-start
  10.0 43.0 %all-gather.2.cloned.1.call-done = bf16[128,4096]{1,0:T(8,128)(2,1)} async-done(((bf16[16,4096]{1,0:T(8,128)(2,1)}), bf16[128,4096]{1,0:T(8,128)(2,1)}) %all-gather.2.cloned.1.call-update) | async-done | bytes 1048592 | tf_op jit(solution)/shard_map/all_gather | solution.py:29
  52.9 0.0 copy-done
  52.9 2.9 %fusion.8 = f32[128,384]{0,1:T(8,128)} fusion(bf16[128,4096]{1,0:T(8,128)(2,1)} %all-gather.2.cloned.1.call-done, bf16[384,4096]{1,0:T(8,128)(2,1)S(1)} %copy-done), kind=kOutput, calls=%fused_computation.10 | convolution fusion | flops 402653184 | bytes 4390912 | tf_op jit(solution)/shard_map/dot_general | solution.py:28
  55.8 0.0 all-reduce.2.cloned.1.call-update
  55.8 17.0 %all-reduce.2.cloned.1.call-done = f32[128,384]{0,1:T(8,128)} async-done(((f32[128,384]{0,1:T(8,128)}), f32[128,384]{0,1:T(8,128)}) %all-reduce.2.cloned.1.call-update) | async-done | bytes 196624 | tf_op jit(solution)/shard_map/psum | solution.py:35
  72.8 1.5 %dynamic-slice_multiply_fusion = f32[128,192]{0,1:T(8,128)} fusion(f32[128,384]{0,1:T(8,128)} %all-reduce.2.cloned.1.call-done, s32[]{:T(128)S(6)} %select_n.3), kind=kLoop, calls=%fused_computation.9 | loop fusion | flops 24576 | bytes 196612 | tf_op jit(solution)/shard_map/mul | solution.py:37
Async XLA Ops:
  6.5 46.4 %copy-start = (bf16[384,4096]{1,0:T(8,128)(2,1)S(1)}, bf16[384,4096]{1,0:T(8,128)(2,1)}, u32[]{:S(2)}) copy-start(bf16[384,4096]{1,0:T(8,128)(2,1)} %param.5) | copy-start | bytes 9437188
  6.5 46.4 %all-gather.2.cloned.1.call-start = ((), (), s32[]{:S(2)}) async-start(), calls=%async_computation | async-start | bytes 1179648 | tf_op jit(solution)/shard_map/all_gather | solution.py:29
  9.9 62.9 %all-reduce.2.cloned.1.call-start = ((), (), s32[]{:S(2)}) async-start(), calls=%async_computation.1 | async-start | bytes 393216 | tf_op jit(solution)/shard_map/psum | solution.py:35
Sparse Core Ops, SparseCore 0:
  10.0 42.8 all-gather.1
  55.9 16.8 all-reduce.1
where the time goes:
time: 81.4 us; the launch traced here: 81.2 us
  waiting for transfers between devices  60 us (74%)
  between operations  13.4 us (16%)
  matrix products  5.53 us (7%)
  other arithmetic  1.54 us (2%)
    all_gather x1, waiting for transfers between devices, shards(): lax.all_gather(precond, 'blk', axis=0, tiled=True)  43 us
    psum x1, waiting for transfers between devices, shards(): summed = lax.psum(terms, 'dim')  17 us
    dot_general x1, matrix products, shards(): lax.dot_general(lax.all_gather(precond, 'blk', axis=0, tiled=True), train...  2.88 us
    dot_general x1, matrix products, precondition(): jnp.einsum('qmc,mbc->qmb', rotated, basis, preferred_element_type=jnp.flo...  2.65 us
  transfers between devices with their start and end apart: 2, of which 2 were waited for; matrix products, arithmetic and copies ran while one was open for 0% of the time, Pallas kernels for 0%

commit v1 on v0

--- a/solution.py
+++ b/solution.py
@@ -1,9 +1,184 @@
+import functools
+
 import jax
 import jax.numpy as jnp
 from jax import lax
+from jax.experimental import pallas as pl
+from jax.experimental.pallas import tpu as pltpu
 from jax.sharding import PartitionSpec as P
 
 PROJ = 8192
+MESH = pl.DeviceIdType.MESH
+X = 2
+Z = 4
+SPLIT = 1536
+
+
+def order(z, s):
+    near = jnp.minimum(z, Z - 1 - z)
+    both = s <= 2 * near
+    side = jnp.where(both, 2 * (s % 2) - 1, jnp.where(2 * z < Z, 1, -1))
+    dist = jnp.where(both, (s + 1) // 2, s - near)
+    return z + side * dist, side
+
+
+def kernel(q_hbm, train_hbm, basis_hbm, inv_hbm, out, buf, train, basis, inv, pq, keep, give, got,
+           load_sem, send_sem, recv_sem, give_sem, got_sem):
+    rows, width = q_hbm.shape
+    half = train_hbm.shape[0] // 2
+    modules, bsz, _ = basis_hbm.shape
+    y, b, d = lax.axis_index("groups"), lax.axis_index("blk"), lax.axis_index("dim")
+    z, x = b // X, b % X
+
+    loads = [pltpu.make_async_copy(basis_hbm, basis, load_sem.at[0]),
+             pltpu.make_async_copy(inv_hbm, inv, load_sem.at[1]),
+             pltpu.make_async_copy(q_hbm, buf.at[z, pl.ds(pl.multiple_of(x * rows, rows), rows)], load_sem.at[2])]
+    for i in range(2):
+        at = pl.multiple_of((d if i == 0 else 1 - d) * half, 16)
+        loads.append(pltpu.make_async_copy(train_hbm.at[pl.ds(at, half)], train.at[i], load_sem.at[3 + i]))
+    for load in loads:
+        load.start()
+
+    up, down = z + 1 < Z, z > 0
+    barrier = pltpu.get_barrier_semaphore()
+
+    def hello(**device):
+        pl.semaphore_signal(barrier, inc=1, device_id=device, device_id_type=MESH)
+
+    hello(blk=z * X + 1 - x)
+    hello(groups=1 - y)
+    hello(dim=1 - d)
+
+    @pl.when(up)
+    def _():
+        hello(blk=b + X)
+
+    @pl.when(down)
+    def _():
+        hello(blk=b - X)
+
+    pl.semaphore_wait(barrier, 3 + jnp.where(up, 1, 0) + jnp.where(down, 1, 0))
+
+    mine = (0, pl.multiple_of(y * SPLIT, 128), SPLIT)
+    other = (1, pl.multiple_of((1 - y) * SPLIT, 128), SPLIT)
+    common = (2, 2 * SPLIT, width - 2 * SPLIT)
+    carried = (mine, common)
+    sends = []
+
+    def place(oz, ox, part):
+        return buf.at[oz, pl.ds(pl.multiple_of(ox * rows, rows), rows), pl.ds(part[1], part[2])]
+
+    def send(cond, oz, ox, part, device, own=False):
+        name = 2 if part[0] == 2 else (y if part[0] == 0 else 1 - y)
+        src = q_hbm.at[:, pl.ds(part[1], part[2])] if own else place(oz, ox, part)
+        copy = pltpu.make_async_remote_copy(
+            src_ref=src, dst_ref=place(oz, ox, part),
+            send_sem=send_sem.at[len(sends)], recv_sem=recv_sem.at[oz * X + ox, name],
+            device_id=device, device_id_type=MESH)
+        sends.append((cond, copy))
+        if cond is None:
+            copy.start()
+        else:
+            pl.when(cond)(copy.start)
+
+    def arrive(oz, ox, part):
+        name = 2 if part[0] == 2 else (y if part[0] == 0 else 1 - y)
+        here = place(oz, ox, part)
+        pltpu.make_async_copy(here, here, recv_sem.at[oz * X + ox, name]).wait()
+
+    for part in carried:
+        send(up, z, x, part, {"blk": b + X}, own=True)
+        send(down, z, x, part, {"blk": b - X}, own=True)
+        send(None, z, x, part, {"blk": z * X + 1 - x}, own=True)
+
+    loads[2].wait()
+    gives = []
+    for s in range(Z):
+        if s + 1 < Z:
+            oz, side = order(z, s + 1)
+            onward = (z - side >= 0) & (z - side < Z)
+            for part in carried:
+                arrive(oz, x, part)
+                send(onward, oz, x, part, {"blk": b - side * X})
+                send(None, oz, x, part, {"blk": z * X + 1 - x})
+                if part[0] == 0:
+                    send(None, oz, x, part, {"groups": 1 - y})
+        oz, _ = order(z, s) if s else (z, None)
+        for part in carried:
+            arrive(oz, 1 - x, part)
+            if part[0] == 0:
+                send(None, oz, 1 - x, part, {"groups": 1 - y})
+        if s:
+            arrive(oz, x, other)
+        arrive(oz, 1 - x, other)
+        if s == 0:
+            loads[0].wait()
+            loads[1].wait()
+        for m in range(modules):
+            cols = slice(m * bsz, (m + 1) * bsz)
+            rot = jnp.dot(buf[oz, :, cols], basis[m], preferred_element_type=jnp.float32) * inv[m:m + 1, :]
+            pre = lax.dot_general(rot.astype(jnp.bfloat16), basis[m], (((1,), (1,)), ((), ())),
+                                  preferred_element_type=jnp.float32)
+            pq[:, cols] = pre.astype(jnp.bfloat16)
+        if s == 0:
+            loads[3].wait()
+            loads[4].wait()
+        there = pl.ds(pl.multiple_of(oz * X * rows, X * rows), X * rows)
+        give[there, :] = lax.dot_general(pq[...], train[1], (((1,), (1,)), ((), ())),
+                                         preferred_element_type=jnp.float32)
+        copy = pltpu.make_async_remote_copy(
+            src_ref=give.at[there], dst_ref=got.at[there], send_sem=give_sem.at[s], recv_sem=got_sem.at[s],
+            device_id={"dim": 1 - d}, device_id_type=MESH)
+        copy.start()
+        gives.append((copy, there))
+        keep[there, :] = lax.dot_general(pq[...], train[0], (((1,), (1,)), ((), ())),
+                                         preferred_element_type=jnp.float32)
+
+    factor = 1.0 / (PROJ ** 0.5)
+    for copy, there in gives:
+        copy.wait_recv()
+        out[there, :] = (keep[there, :] + got[there, :]) * factor
+    for cond, copy in sends:
+        if cond is None:
+            copy.wait_send()
+        else:
+            pl.when(cond)(copy.wait_send)
+    for copy, _ in gives:
+        copy.wait_send()
+
+
+def fused(queries, train_proj, basis, inv_eigen):
+    rows, width = queries.shape
+    examples = train_proj.shape[0]
+    total = rows * X * Z
+    half = (total, examples // 2)
+    hbm = pl.BlockSpec(memory_space=pl.ANY)
+    vmem = pl.BlockSpec(memory_space=pltpu.VMEM)
+    return pl.pallas_call(
+        kernel,
+        out_shape=jax.ShapeDtypeStruct(half, jnp.float32),
+        in_specs=[hbm] * 4,
+        out_specs=vmem,
+        scratch_shapes=[
+            pltpu.VMEM((Z, X * rows, width), jnp.bfloat16),
+            pltpu.VMEM((2, examples // 2, width), jnp.bfloat16),
+            pltpu.VMEM(basis.shape, basis.dtype),
+            pltpu.VMEM(inv_eigen.shape, inv_eigen.dtype),
+            pltpu.VMEM((X * rows, width), jnp.bfloat16),
+            pltpu.VMEM(half, jnp.float32),
+            pltpu.VMEM(half, jnp.float32),
+            pltpu.VMEM(half, jnp.float32),
+            pltpu.SemaphoreType.DMA((5,)),
+            pltpu.SemaphoreType.DMA((40,)),
+            pltpu.SemaphoreType.DMA((X * Z, 3)),
+            pltpu.SemaphoreType.DMA((Z,)),
+            pltpu.SemaphoreType.DMA((Z,)),
+        ],
+        compiler_params=pltpu.CompilerParams(
+            collective_id=0, has_side_effects=True, vmem_limit_bytes=48 * 1024 * 1024),
+        cost_estimate=pl.CostEstimate(flops=2 * total * width * (examples + 256), transcendentals=0,
+                                      bytes_accessed=2 * width * (examples + 256)),
+    )(queries, train_proj, basis, inv_eigen)
 
 
 def precondition(queries, basis, inv_eigen):
@@ -39,8 +214,9 @@
 
 def solution(mesh):
     placed = (P("blk", "dim"), P(("groups", "blk"), "dim"), P("dim", None, None), P("dim", None))
+    small = mesh.shape["blk"] == X * Z and mesh.shape["groups"] == 2 and mesh.shape["dim"] == 2
     return jax.shard_map(
-        shards,
+        fused if small else shards,
         mesh=mesh,
         in_specs=placed,
         out_specs=P(None, ("groups", "blk", "dim")),

time: 81.4 us -> 47.4 us (0.58)
  waiting for transfers between devices: 60 us -> 0 us
  Pallas kernels: 0 us -> 41.6 us
  between operations: 13.4 us -> 0.01 us
  matrix products: 5.53 us -> 0 us
  local copies, waits for them, and re-layouts: 0.69 us -> 5.47 us
  other arithmetic: 1.54 us -> 0 us
    all_gather x1 -> x0, waiting for transfers between devices: 43 us -> none  [shards(): lax.all_gather(precond, 'blk', axis=0, tiled=True)]
    pallas_call x0 -> x1, Pallas kernels: none -> 41.6 us  [fused(): pl.pallas_call(kernel, out_shape=jax.ShapeDtypeStruct(half, jnp.float32),...]
    psum x1 -> x0, waiting for transfers between devices: 17 us -> none  [shards(): summed = lax.psum(terms, 'dim')]
    dot_general x2 -> x0, matrix products: 5.53 us -> none  [the longest x1 2.88 us: shards(): lax.dot_general(lax.all_gather(precond, 'blk', axis=0, tiled=True), train...]
    unnamed x2 -> x8, local copies, waits for them, and re-layouts: 0.01 us -> 4.73 us
    mul x1 -> x0, other arithmetic: 1.54 us -> none  [shards(): return own * factor]
  transfers between devices with their start and end apart: 2 -> 0, of which waited for: 2 -> 0; matrix products, arithmetic and copies ran while one was open for 0% -> 0% of each run, Pallas kernels for 0% -> 0%
where the time goes in v1:
time: 47.4 us; the launch traced here: 47.1 us
  Pallas kernels  41.6 us (88%)
  local copies, waits for them, and re-layouts  5.47 us (12%)
    pallas_call x1, Pallas kernels, fused(): pl.pallas_call(kernel, out_shape=jax.ShapeDtypeStruct(half, jnp.float32),...  41.6 us
    unnamed x8, local copies, waits for them, and re-layouts  4.73 us

profile of v1, /device:TPU:0, one launch (start us, length us, event | category | flops | bytes accessed | tf_op | source)
XLA Modules:
  0.0 47.1 jit_solution(2340135181258855732)
XLA Ops:
  0.0 0.0 copy-start
  0.0 1.9 %copy-done = bf16[384,4096]{1,0:T(8,128)(2,1)S(1)} copy-done((bf16[384,4096]{1,0:T(8,128)(2,1)S(1)}, bf16[384,4096]{1,0:T(8,128)(2,1)}, u32[]{:S(2)}) %copy-start) | copy-done | bytes 3145752
  1.9 0.0 copy-start.1
  1.9 1.2 %copy-done.1 = bf16[32,128,128]{2,1,0:T(8,128)(2,1)S(1)} copy-done((bf16[32,128,128]{2,1,0:T(8,128)(2,1)S(1)}, bf16[32,128,128]{2,1,0:T(8,128)(2,1)}, u32[]{:S(2)}) %copy-start.1) | copy-done | bytes 1048600
  3.1 0.0 copy-start.2
  3.1 0.9 %copy-done.2 = bf16[16,4096]{1,0:T(8,128)(2,1)S(1)} copy-done((bf16[16,4096]{1,0:T(8,128)(2,1)S(1)}, bf16[16,4096]{1,0:T(8,128)(2,1)}, u32[]{:S(2)}) %copy-start.2) | copy-done | bytes 131096
  4.0 0.0 copy-start.3
  4.0 0.7 %copy-done.3 = f32[32,128]{1,0:T(8,128)S(1)} copy-done((f32[32,128]{1,0:T(8,128)S(1)}, f32[32,128]{1,0:T(8,128)}, u32[]{:S(2)}) %copy-start.3) | copy-done | bytes 16408
  4.7 41.6 %shard_map.46 = f32[128,192]{1,0:T(8,128)S(1)} custom-call(bf16[16,4096]{1,0:T(8,128)(2,1)S(1)} %copy-done.2, bf16[384,4096]{1,0:T(8,128)(2,1)S(1)} %copy-done, bf16[32,128,128]{2,1,0:T(8,128)(2,1)S(1)} %copy-done.1, f32[32,128]{1,0:T(8,128)S(1)} %copy-done.3), custom_call_target="tpu_custom_call" | custom-call | flops 671088640 | bytes 5242880 | tf_op jit(solution)/shard_map/pallas_call | solution.py:157
  46.4 0.7 %copy.5 = f32[128,192]{0,1:T(8,128)} copy(f32[128,192]{1,0:T(8,128)S(1)} %shard_map.46) | data formatting | bytes 196608 | tf_op jit(solution)/shard_map/pallas_call | solution.py:157
Async XLA Ops:
  0.0 1.9 %copy-start = (bf16[384,4096]{1,0:T(8,128)(2,1)S(1)}, bf16[384,4096]{1,0:T(8,128)(2,1)}, u32[]{:S(2)}) copy-start(bf16[384,4096]{1,0:T(8,128)(2,1)} %train_hbm.1) | copy-start | bytes 9437188
  1.9 1.2 %copy-start.1 = (bf16[32,128,128]{2,1,0:T(8,128)(2,1)S(1)}, bf16[32,128,128]{2,1,0:T(8,128)(2,1)}, u32[]{:S(2)}) copy-start(bf16[32,128,128]{2,1,0:T(8,128)(2,1)} %basis_hbm.1) | copy-start | bytes 3145732
  3.1 0.9 %copy-start.2 = (bf16[16,4096]{1,0:T(8,128)(2,1)S(1)}, bf16[16,4096]{1,0:T(8,128)(2,1)}, u32[]{:S(2)}) copy-start(bf16[16,4096]{1,0:T(8,128)(2,1)} %q_hbm.1) | copy-start | bytes 393220
  4.0 0.7 %copy-start.3 = (f32[32,128]{1,0:T(8,128)S(1)}, f32[32,128]{1,0:T(8,128)}, u32[]{:S(2)}) copy-start(f32[32,128]{1,0:T(8,128)} %inv_hbm.1) | copy-start | bytes 49156

commit v2 on v0

--- a/solution.py
+++ b/solution.py
@@ -1,9 +1,179 @@
+import functools
+
 import jax
 import jax.numpy as jnp
 from jax import lax
+from jax.experimental import pallas as pl
+from jax.experimental.pallas import tpu as pltpu
 from jax.sharding import PartitionSpec as P
 
 PROJ = 8192
+MESH = pl.DeviceIdType.MESH
+X = 2
+Z = 4
+SPLIT = 1536
+
+
+def order(z, s):
+    near = jnp.minimum(z, Z - 1 - z)
+    both = s <= 2 * near
+    side = jnp.where(both, 2 * (s % 2) - 1, jnp.where(2 * z < Z, 1, -1))
+    dist = jnp.where(both, (s + 1) // 2, s - near)
+    return z + side * dist, side
+
+
+def kernel(q_hbm, train_hbm, basis_hbm, inv_hbm, out, q, rot, buf, train, basis, inv, keep, give, got,
+           load_sem, send_sem, recv_sem, give_sem, got_sem):
+    rows, width = q_hbm.shape
+    half = train_hbm.shape[0] // 2
+    bsz = basis_hbm.shape[1]
+    y, b, d = lax.axis_index("groups"), lax.axis_index("blk"), lax.axis_index("dim")
+    z, x = b // X, b % X
+    planes = [order(z, s)[0] for s in range(1, Z)]
+
+    barrier = pltpu.get_barrier_semaphore()
+
+    def hello(**device):
+        pl.semaphore_signal(barrier, inc=1, device_id=device, device_id_type=MESH)
+
+    hello(blk=z * X + 1 - x)
+    hello(groups=1 - y)
+    hello(dim=1 - d)
+    for oz in planes:
+        hello(blk=oz * X + x)
+
+    loads = [pltpu.make_async_copy(basis_hbm, basis, load_sem.at[0]),
+             pltpu.make_async_copy(inv_hbm, inv, load_sem.at[1]),
+             pltpu.make_async_copy(q_hbm, q, load_sem.at[2])]
+    for i in range(2):
+        at = pl.multiple_of((d if i == 0 else 1 - d) * half, 16)
+        loads.append(pltpu.make_async_copy(train_hbm.at[pl.ds(at, half)], train.at[i], load_sem.at[3 + i]))
+    for load in loads:
+        load.start()
+
+    mine = (y * SPLIT, SPLIT, y)
+    other = ((1 - y) * SPLIT, SPLIT, 1 - y)
+    common = (2 * SPLIT, width - 2 * SPLIT, 2)
+    sends = []
+
+    def columns(part):
+        start = part[0] if isinstance(part[0], int) else pl.multiple_of(part[0], 128)
+        return pl.ds(start, part[1])
+
+    def lines(oz, ox):
+        return pl.ds(pl.multiple_of((oz * X + ox) * rows, rows), rows)
+
+    def send(oz, ox, part, device):
+        place = buf.at[lines(oz, ox), columns(part)]
+        copy = pltpu.make_async_remote_copy(
+            src_ref=place, dst_ref=place,
+            send_sem=send_sem.at[len(sends)], recv_sem=recv_sem.at[oz * X + ox, part[2]],
+            device_id=device, device_id_type=MESH)
+        copy.start()
+        sends.append(copy)
+
+    def arrive(oz, ox, part):
+        place = buf.at[lines(oz, ox), columns(part)]
+        pltpu.make_async_copy(place, place, recv_sem.at[oz * X + ox, part[2]]).wait()
+
+    def precondition_own(part):
+        for i in range(part[1] // bsz):
+            m = part[0] // bsz + i
+            cols = columns((part[0] + i * bsz, bsz))
+            first = jnp.dot(q[:, cols], basis[m], preferred_element_type=jnp.float32)
+            rot[:, i * bsz:(i + 1) * bsz] = (first * inv[pl.ds(m, 1), :]).astype(jnp.bfloat16)
+        for i in range(part[1] // bsz):
+            m = part[0] // bsz + i
+            second = lax.dot_general(rot[:, i * bsz:(i + 1) * bsz], basis[m], (((1,), (1,)), ((), ())),
+                                     preferred_element_type=jnp.float32)
+            buf[lines(z, x), columns((part[0] + i * bsz, bsz))] = second.astype(jnp.bfloat16)
+
+    for load in loads[:3]:
+        load.wait()
+    precondition_own(mine)
+    pl.semaphore_wait(barrier, Z + 2)
+    for part in (mine, common):
+        if part is common:
+            precondition_own(common)
+        send(z, x, part, {"blk": z * X + 1 - x})
+        for oz in planes:
+            send(z, x, part, {"blk": oz * X + x})
+    precondition_own(other)
+
+    def hand_over(oz):
+        for part in (mine, common):
+            arrive(oz, 1 - x, part)
+            if part is mine:
+                send(oz, 1 - x, part, {"groups": 1 - y})
+
+    hand_over_next = z
+    for oz in planes:
+        for part in (mine, common):
+            arrive(oz, x, part)
+            send(oz, x, part, {"blk": z * X + 1 - x})
+            if part is mine:
+                send(oz, x, part, {"groups": 1 - y})
+        hand_over(hand_over_next)
+        hand_over_next = oz
+    hand_over(hand_over_next)
+
+    def score(i, part):
+        return lax.dot_general(buf[:, columns(part)], train[i, :, columns(part)], (((1,), (1,)), ((), ())),
+                               preferred_element_type=jnp.float32)
+
+    loads[3].wait()
+    loads[4].wait()
+    give[...] = score(1, mine) + score(1, common)
+    keep[...] = score(0, mine) + score(0, common)
+    arrive(z, 1 - x, other)
+    for oz in planes:
+        arrive(oz, x, other)
+        arrive(oz, 1 - x, other)
+    give[...] += score(1, other)
+    swap = pltpu.make_async_remote_copy(src_ref=give, dst_ref=got, send_sem=give_sem, recv_sem=got_sem,
+                                        device_id={"dim": 1 - d}, device_id_type=MESH)
+    swap.start()
+    keep[...] += score(0, other)
+    swap.wait_recv()
+    out[...] = (keep[...] + got[...]) * (1.0 / (PROJ ** 0.5))
+    for copy in sends:
+        copy.wait_send()
+    swap.wait_send()
+
+
+def fused(queries, train_proj, basis, inv_eigen):
+    rows, width = queries.shape
+    examples = train_proj.shape[0]
+    total = rows * X * Z
+    half = (total, examples // 2)
+    hbm = pl.BlockSpec(memory_space=pl.ANY)
+    vmem = pl.BlockSpec(memory_space=pltpu.VMEM)
+    return pl.pallas_call(
+        kernel,
+        out_shape=jax.ShapeDtypeStruct(half, jnp.float32),
+        in_specs=[hbm] * 4,
+        out_specs=vmem,
+        scratch_shapes=[
+            pltpu.VMEM((rows, width), jnp.bfloat16),
+            pltpu.VMEM((rows, width), jnp.bfloat16),
+            pltpu.VMEM((total, width), jnp.bfloat16),
+            pltpu.VMEM((2, examples // 2, width), jnp.bfloat16),
+            pltpu.VMEM(basis.shape, basis.dtype),
+            pltpu.VMEM(inv_eigen.shape, inv_eigen.dtype),
+            pltpu.VMEM(half, jnp.float32),
+            pltpu.VMEM(half, jnp.float32),
+            pltpu.VMEM(half, jnp.float32),
+            pltpu.SemaphoreType.DMA((5,)),
+            pltpu.SemaphoreType.DMA((2 * Z + 3 * (Z - 1) + Z,)),
+            pltpu.SemaphoreType.DMA((X * Z, 3)),
+            pltpu.SemaphoreType.DMA,
+            pltpu.SemaphoreType.DMA,
+        ],
+        compiler_params=pltpu.CompilerParams(
+            collective_id=0, has_side_effects=True, vmem_limit_bytes=60 * 1024 * 1024),
+        cost_estimate=pl.CostEstimate(flops=2 * total * width * (examples + 256), transcendentals=0,
+                                      bytes_accessed=2 * width * (examples + 256)),
+    )(queries, train_proj, basis, inv_eigen)
 
 
 def precondition(queries, basis, inv_eigen):
@@ -39,8 +209,9 @@
 
 def solution(mesh):
     placed = (P("blk", "dim"), P(("groups", "blk"), "dim"), P("dim", None, None), P("dim", None))
+    small = mesh.shape["blk"] == X * Z and mesh.shape["groups"] == 2 and mesh.shape["dim"] == 2
     return jax.shard_map(
-        shards,
+        fused if small else shards,
         mesh=mesh,
         in_specs=placed,
         out_specs=P(None, ("groups", "blk", "dim")),

time: 81.4 us -> 25.3 us (0.31)
  waiting for transfers between devices: 60 us -> 0 us
  Pallas kernels: 0 us -> 23.5 us
  between operations: 13.4 us -> 0.01 us
  matrix products: 5.53 us -> 0 us
  other arithmetic: 1.54 us -> 0 us
  local copies, waits for them, and re-layouts: 0.69 us -> 1.64 us
    all_gather x1 -> x0, waiting for transfers between devices: 43 us -> none  [shards(): lax.all_gather(precond, 'blk', axis=0, tiled=True)]
    pallas_call x0 -> x1, Pallas kernels: none -> 23.5 us  [fused(): pl.pallas_call(kernel, out_shape=jax.ShapeDtypeStruct(half, jnp.float32),...]
    psum x1 -> x0, waiting for transfers between devices: 17 us -> none  [shards(): summed = lax.psum(terms, 'dim')]
    dot_general x2 -> x0, matrix products: 5.53 us -> none  [the longest x1 2.88 us: shards(): lax.dot_general(lax.all_gather(precond, 'blk', axis=0, tiled=True), train...]
    pallas_call x0 -> x1, local copies, waits for them, and re-layouts: none -> 1.64 us  [fused(): pl.pallas_call(kernel, out_shape=jax.ShapeDtypeStruct(half, jnp.float32),...]
    mul x1 -> x0, other arithmetic: 1.54 us -> none  [shards(): return own * factor]
  transfers between devices with their start and end apart: 2 -> 0, of which waited for: 2 -> 0; matrix products, arithmetic and copies ran while one was open for 0% -> 0% of each run, Pallas kernels for 0% -> 0%
where the time goes in v2:
time: 25.3 us; the launch traced here: 25.1 us
  Pallas kernels  23.5 us (93%)
  local copies, waits for them, and re-layouts  1.64 us (6%)
    pallas_call x1, Pallas kernels, fused(): pl.pallas_call(kernel, out_shape=jax.ShapeDtypeStruct(half, jnp.float32),...  23.5 us
    pallas_call x1, local copies, waits for them, and re-layouts, fused(): pl.pallas_call(kernel, out_shape=jax.ShapeDtypeStruct(half, jnp.float32),...  1.64 us

profile of v2, /device:TPU:0, one launch (start us, length us, event | category | flops | bytes accessed | tf_op | source)
XLA Modules:
  0.0 25.1 jit_solution(17117118932030871727)
XLA Ops:
  0.0 23.5 %shard_map.46 = f32[128,192]{1,0:T(8,128)} custom-call(bf16[16,4096]{1,0:T(8,128)(2,1)} %q_hbm.1, bf16[384,4096]{1,0:T(8,128)(2,1)} %train_hbm.1, bf16[32,128,128]{2,1,0:T(8,128)(2,1)} %basis_hbm.1, f32[32,128]{1,0:T(8,128)} %inv_hbm.1), custom_call_target="tpu_custom_call" | custom-call | flops 671088640 | bytes 5242880 | tf_op jit(solution)/shard_map/pallas_call | solution.py:151
  23.5 1.6 %copy.5 = f32[128,192]{0,1:T(8,128)} copy(f32[128,192]{1,0:T(8,128)} %shard_map.46) | data formatting | bytes 196608 | tf_op jit(solution)/shard_map/pallas_call | solution.py:151

commit v3 on v2

--- a/solution.py
+++ b/solution.py
@@ -11,7 +11,6 @@
 MESH = pl.DeviceIdType.MESH
 X = 2
 Z = 4
-SPLIT = 1536
 
 
 def order(z, s):
@@ -51,9 +50,10 @@
     for load in loads:
         load.start()
 
-    mine = (y * SPLIT, SPLIT, y)
-    other = ((1 - y) * SPLIT, SPLIT, 1 - y)
-    common = (2 * SPLIT, width - 2 * SPLIT, 2)
+    split = width // 2
+    mine = (y * split, split, y)
+    other = ((1 - y) * split, split, 1 - y)
+    whole = (0, width, 2)
     sends = []
 
     def columns(part):
@@ -92,30 +92,23 @@
         load.wait()
     precondition_own(mine)
     pl.semaphore_wait(barrier, Z + 2)
-    for part in (mine, common):
-        if part is common:
-            precondition_own(common)
-        send(z, x, part, {"blk": z * X + 1 - x})
-        for oz in planes:
-            send(z, x, part, {"blk": oz * X + x})
+    for oz in planes:
+        send(z, x, mine, {"blk": oz * X + x})
     precondition_own(other)
+    send(z, x, whole, {"blk": z * X + 1 - x})
 
     def hand_over(oz):
-        for part in (mine, common):
-            arrive(oz, 1 - x, part)
-            if part is mine:
-                send(oz, 1 - x, part, {"groups": 1 - y})
-
-    hand_over_next = z
-    for oz in planes:
-        for part in (mine, common):
-            arrive(oz, x, part)
-            send(oz, x, part, {"blk": z * X + 1 - x})
-            if part is mine:
-                send(oz, x, part, {"groups": 1 - y})
-        hand_over(hand_over_next)
-        hand_over_next = oz
-    hand_over(hand_over_next)
+        arrive(oz, 1 - x, mine)
+        send(oz, 1 - x, mine, {"groups": 1 - y})
+
+    for s, oz in enumerate(planes):
+        arrive(oz, x, mine)
+        send(oz, x, mine, {"groups": 1 - y})
+        send(oz, x, mine, {"blk": z * X + 1 - x})
+        if s:
+            hand_over(planes[s - 1])
+    hand_over(planes[-1])
+    arrive(z, 1 - x, whole)
 
     def score(i, part):
         return lax.dot_general(buf[:, columns(part)], train[i, :, columns(part)], (((1,), (1,)), ((), ())),
@@ -123,9 +116,8 @@
 
     loads[3].wait()
     loads[4].wait()
-    give[...] = score(1, mine) + score(1, common)
-    keep[...] = score(0, mine) + score(0, common)
-    arrive(z, 1 - x, other)
+    give[...] = score(1, mine)
+    keep[...] = score(0, mine)
     for oz in planes:
         arrive(oz, x, other)
         arrive(oz, 1 - x, other)
@@ -164,7 +156,7 @@
             pltpu.VMEM(half, jnp.float32),
             pltpu.VMEM(half, jnp.float32),
             pltpu.SemaphoreType.DMA((5,)),
-            pltpu.SemaphoreType.DMA((2 * Z + 3 * (Z - 1) + Z,)),
+            pltpu.SemaphoreType.DMA((4 * Z,)),
             pltpu.SemaphoreType.DMA((X * Z, 3)),
             pltpu.SemaphoreType.DMA,
             pltpu.SemaphoreType.DMA,

time: 25.3 us -> 24.7 us (0.976)
  Pallas kernels: 23.5 us -> 22.9 us
    pallas_call x1, Pallas kernels: 23.5 us -> 22.9 us  [fused(): pl.pallas_call(kernel, out_shape=jax.ShapeDtypeStruct(half, jnp.float32),...]
where the time goes in v3:
time: 24.7 us; the launch traced here: 24.6 us
  Pallas kernels  22.9 us (93%)
  local copies, waits for them, and re-layouts  1.64 us (7%)
    pallas_call x1, Pallas kernels, fused(): pl.pallas_call(kernel, out_shape=jax.ShapeDtypeStruct(half, jnp.float32),...  22.9 us
    pallas_call x1, local copies, waits for them, and re-layouts, fused(): pl.pallas_call(kernel, out_shape=jax.ShapeDtypeStruct(half, jnp.float32),...  1.64 us

profile of v3, /device:TPU:0, one launch (start us, length us, event | category | flops | bytes accessed | tf_op | source)
XLA Modules:
  0.0 24.6 jit_solution(10769003766934343729)
XLA Ops:
  0.0 22.9 %shard_map.46 = f32[128,192]{1,0:T(8,128)} custom-call(bf16[16,4096]{1,0:T(8,128)(2,1)} %q_hbm.1, bf16[384,4096]{1,0:T(8,128)(2,1)} %train_hbm.1, bf16[32,128,128]{2,1,0:T(8,128)(2,1)} %basis_hbm.1, f32[32,128]{1,0:T(8,128)} %inv_hbm.1), custom_call_target="tpu_custom_call" | custom-call | flops 671088640 | bytes 5242880 | tf_op jit(solution)/shard_map/pallas_call | solution.py:143
  22.9 1.6 %copy.5 = f32[128,192]{0,1:T(8,128)} copy(f32[128,192]{1,0:T(8,128)} %shard_map.46) | data formatting | bytes 196608 | tf_op jit(solution)/shard_map/pallas_call | solution.py:143

commit v4 on v3

--- a/solution.py
+++ b/solution.py
@@ -101,13 +101,15 @@
         arrive(oz, 1 - x, mine)
         send(oz, 1 - x, mine, {"groups": 1 - y})
 
-    for s, oz in enumerate(planes):
+    for oz in planes:
         arrive(oz, x, mine)
         send(oz, x, mine, {"groups": 1 - y})
         send(oz, x, mine, {"blk": z * X + 1 - x})
-        if s:
-            hand_over(planes[s - 1])
-    hand_over(planes[-1])
+    arrive(planes[0], x, other)
+    send(planes[0], x, other, {"blk": z * X + 1 - x})
+    for oz in planes[1:]:
+        hand_over(oz)
+    arrive(planes[0], 1 - x, mine)
     arrive(z, 1 - x, whole)
 
     def score(i, part):
@@ -119,7 +121,8 @@
     give[...] = score(1, mine)
     keep[...] = score(0, mine)
     for oz in planes:
-        arrive(oz, x, other)
+        if oz is not planes[0]:
+            arrive(oz, x, other)
         arrive(oz, 1 - x, other)
     give[...] += score(1, other)
     swap = pltpu.make_async_remote_copy(src_ref=give, dst_ref=got, send_sem=give_sem, recv_sem=got_sem,

time: 24.7 us -> 24.7 us (level)
  no operation moved by 1% of the time
where the time goes in v4:
time: 24.7 us; the launch traced here: 24.6 us
  Pallas kernels  22.9 us (93%)
  local copies, waits for them, and re-layouts  1.64 us (7%)
    pallas_call x1, Pallas kernels, fused(): pl.pallas_call(kernel, out_shape=jax.ShapeDtypeStruct(half, jnp.float32),...  22.9 us
    pallas_call x1, local copies, waits for them, and re-layouts, fused(): pl.pallas_call(kernel, out_shape=jax.ShapeDtypeStruct(half, jnp.float32),...  1.64 us

profile of v4, /device:TPU:0, one launch (start us, length us, event | category | flops | bytes accessed | tf_op | source)
XLA Modules:
  0.0 24.6 jit_solution(10995374854155668631)
XLA Ops:
  0.0 22.9 %shard_map.46 = f32[128,192]{1,0:T(8,128)} custom-call(bf16[16,4096]{1,0:T(8,128)(2,1)} %q_hbm.1, bf16[384,4096]{1,0:T(8,128)(2,1)} %train_hbm.1, bf16[32,128,128]{2,1,0:T(8,128)(2,1)} %basis_hbm.1, f32[32,128]{1,0:T(8,128)} %inv_hbm.1), custom_call_target="tpu_custom_call" | custom-call | flops 671088640 | bytes 5242880 | tf_op jit(solution)/shard_map/pallas_call | solution.py:146
  22.9 1.6 %copy.5 = f32[128,192]{0,1:T(8,128)} copy(f32[128,192]{1,0:T(8,128)} %shard_map.46) | data formatting | bytes 196608 | tf_op jit(solution)/shard_map/pallas_call | solution.py:146

commit v5 on v4

--- a/solution.py
+++ b/solution.py
@@ -124,16 +124,25 @@
         if oz is not planes[0]:
             arrive(oz, x, other)
         arrive(oz, 1 - x, other)
-    give[...] += score(1, other)
-    swap = pltpu.make_async_remote_copy(src_ref=give, dst_ref=got, send_sem=give_sem, recv_sem=got_sem,
-                                        device_id={"dim": 1 - d}, device_id_type=MESH)
-    swap.start()
+    swaps = []
+    count = give.shape[0] // 2
+    for i in range(2):
+        top = slice(i * count, (i + 1) * count)
+        give[top, :] += lax.dot_general(buf[top, columns(other)], train[1, :, columns(other)],
+                                        (((1,), (1,)), ((), ())), preferred_element_type=jnp.float32)
+        here = pl.ds(i * count, count)
+        swaps.append(pltpu.make_async_remote_copy(
+            src_ref=give.at[here], dst_ref=got.at[here], send_sem=give_sem.at[i], recv_sem=got_sem.at[i],
+            device_id={"dim": 1 - d}, device_id_type=MESH))
+        swaps[i].start()
     keep[...] += score(0, other)
-    swap.wait_recv()
+    for swap in swaps:
+        swap.wait_recv()
     out[...] = (keep[...] + got[...]) * (1.0 / (PROJ ** 0.5))
     for copy in sends:
         copy.wait_send()
-    swap.wait_send()
+    for swap in swaps:
+        swap.wait_send()
 
 
 def fused(queries, train_proj, basis, inv_eigen):
@@ -161,8 +170,8 @@
             pltpu.SemaphoreType.DMA((5,)),
             pltpu.SemaphoreType.DMA((4 * Z,)),
             pltpu.SemaphoreType.DMA((X * Z, 3)),
-            pltpu.SemaphoreType.DMA,
-            pltpu.SemaphoreType.DMA,
+            pltpu.SemaphoreType.DMA((2,)),
+            pltpu.SemaphoreType.DMA((2,)),
         ],
         compiler_params=pltpu.CompilerParams(
             collective_id=0, has_side_effects=True, vmem_limit_bytes=60 * 1024 * 1024),

time: 24.7 us -> 25.2 us (1.020)
  Pallas kernels: 22.9 us -> 23.4 us
    pallas_call x1, Pallas kernels: 22.9 us -> 23.4 us  [fused(): pl.pallas_call(kernel, out_shape=jax.ShapeDtypeStruct(half, jnp.float32),...]
where the time goes in v5:
time: 25.2 us; the launch traced here: 25 us
  Pallas kernels  23.4 us (93%)
  local copies, waits for them, and re-layouts  1.64 us (7%)
    pallas_call x1, Pallas kernels, fused(): pl.pallas_call(kernel, out_shape=jax.ShapeDtypeStruct(half, jnp.float32),...  23.4 us
    pallas_call x1, local copies, waits for them, and re-layouts, fused(): pl.pallas_call(kernel, out_shape=jax.ShapeDtypeStruct(half, jnp.float32),...  1.64 us

profile of v5, /device:TPU:0, one launch (start us, length us, event | category | flops | bytes accessed | tf_op | source)
XLA Modules:
  0.0 25.0 jit_solution(4976459062837816321)
XLA Ops:
  0.0 23.4 %shard_map.46 = f32[128,192]{1,0:T(8,128)} custom-call(bf16[16,4096]{1,0:T(8,128)(2,1)} %q_hbm.1, bf16[384,4096]{1,0:T(8,128)(2,1)} %train_hbm.1, bf16[32,128,128]{2,1,0:T(8,128)(2,1)} %basis_hbm.1, f32[32,128]{1,0:T(8,128)} %inv_hbm.1), custom_call_target="tpu_custom_call" | custom-call | flops 671088640 | bytes 5242880 | tf_op jit(solution)/shard_map/pallas_call | solution.py:155
  23.4 1.6 %copy.5 = f32[128,192]{0,1:T(8,128)} copy(f32[128,192]{1,0:T(8,128)} %shard_map.46) | data formatting | bytes 196608 | tf_op jit(solution)/shard_map/pallas_call | solution.py:155
